TPU v7x, 32 devices: a whole 2x2x4 slice. The times are simulated.
32 devices in a mesh: node: 16 (over z, y, x), head: 2 (over core).
Axes of the slice: x: 2, y: 2, z: 4, core: 2. Of those that a mesh axis runs over, the one named last changes fastest.
Arguments:
- features: bfloat16 [2048, 128], P('node'), may hold values from -1201 to 1201
- proj_weight: bfloat16 [128, 1024], P(None, 'head'), may hold values from -1 to 1
- score_source: float32 [8, 128], P('head'), may hold values from -1 to 1
- score_target: float32 [8, 128], P('head'), may hold values from -1 to 1
- out_weight: bfloat16 [1024, 256], P('head'), may hold values from -0.1875 to 0.1875
- presence: int32 [16, 16], P('node'), may hold values from 0 to 1, as said below
- tile_masks: int32 [16, 4, 128, 128], P('node'), may hold values 0 or 1
Outputs:
- mixed: bfloat16 [2048, 256], P('node')
Inputs may be any that keep to these rules, and one draw needn't show every extreme that they name: Each row holds exactly 4 ones; tile_masks[r, k] belongs to the k-th present tile of row r of presence, counted in ascending order of tile.
All inputs are finite; a program needn't handle non-finite values. No bound on the sum of `tile_masks` on one device may be relied on, other than what follows from the above.
Results may differ from a plain program's by a relative error of at most 0.015.
Values may be sent and summed in bfloat16 or wider, within the bound.
A program may use at most 64 MiB of HBM per device.

v0:
```python
import functools

import jax
import jax.numpy as jnp
from jax import lax
from jax.experimental import pallas as pl
from jax.experimental.pallas import tpu as pltpu
from jax.sharding import PartitionSpec as P

MESH = pl.DeviceIdType.MESH
CUT = -1e30
F32 = jnp.float32
BF16 = jnp.bfloat16
ACROSS = (((1,), (1,)), ((), ()))


def leaky_relu(values):
    return jnp.maximum(values, 0.2 * values)


def elu(values):
    low = jnp.minimum(values, 0.0)
    near = low * (1.0 + low * (0.5 + low * (1.0 / 6.0)))
    far = jnp.exp(low) - 1.0
    return jnp.where(values > 0, values, jnp.where(low > -0.015625, near, far))


def split_rows(values):
    high = values.astype(BF16).astype(F32)
    rest = values - high
    middle = rest.astype(BF16).astype(F32)
    low = rest - middle
    return jnp.concatenate([high, middle, low, jnp.zeros_like(low)], axis=0).astype(BF16)


def kernel(
    sizes,
    features,
    proj_weight,
    score_source,
    score_target,
    out_weight,
    presence,
    tile_masks,
    result,
    gathered,
    own_buf,
    proj_buf,
    score_buf,
    out_buf,
    presence_buf,
    mask_buf,
    cut_buf,
    vectors,
    own_proj,
    projected,
    source_proj,
    partials,
    local_sem,
    outer_send,
    outer_recv,
    inner_send,
    inner_recv,
    group_send,
    group_recv,
    part_send,
    part_recv,
):
    outer, inner, heads_dev, heads, width, tile, slots = sizes
    nodes = outer * inner
    pad = vectors.shape[1]
    me = lax.axis_index("node")
    my_head = lax.axis_index("head")
    my_outer = me // inner
    my_inner = me % inner
    share = tile // heads_dev

    def outer_peer(step):
        return lax.rem(my_outer + step, outer) * inner + my_inner

    def inner_peer(step):
        return my_outer * inner + lax.rem(my_inner + step, inner)

    def head_peer(step):
        return lax.rem(my_head + step, heads_dev)

    barrier = pltpu.get_barrier_semaphore()
    for step in range(1, outer):
        pl.semaphore_signal(barrier, inc=1, device_id=(outer_peer(step), my_head), device_id_type=MESH)
    for step in range(1, inner):
        pl.semaphore_signal(barrier, inc=1, device_id=(inner_peer(step), my_head), device_id_type=MESH)
    for step in range(1, heads_dev):
        pl.semaphore_signal(barrier, inc=1, device_id=(me, head_peer(step)), device_id_type=MESH)

    own_share = features.at[pl.ds(pl.multiple_of(my_head * share, share), share), :]
    loads = []
    for source, target in (
        (features, own_buf),
        (proj_weight, proj_buf),
        (score_source, score_buf.at[0]),
        (score_target, score_buf.at[1]),
        (presence, presence_buf),
        (tile_masks.at[0], mask_buf),
        (own_share, gathered.at[my_head, me]),
        (out_weight, out_buf),
    ):
        load = pltpu.make_async_copy(source, target, local_sem.at[len(loads)])
        load.start()
        loads.append(load)
    pl.semaphore_wait(barrier, outer + inner + heads_dev - 3)

    started = []

    def send(source, target, to, send_sem, recv_sem):
        copy = pltpu.make_async_remote_copy(
            src_ref=source,
            dst_ref=target,
            send_sem=send_sem,
            recv_sem=recv_sem,
            device_id=to,
            device_id_type=MESH,
        )
        copy.start()
        started.append(copy)

    def origin_outer(hop):
        return lax.rem(my_outer + outer - hop, outer)

    def origin(hop, step):
        return origin_outer(hop) * inner + lax.rem(my_inner + inner - step, inner)

    def to_inner(hop, source):
        for step in range(1, inner):
            send(
                source,
                gathered.at[my_head, origin(hop, 0)],
                (inner_peer(step), my_head),
                inner_send.at[hop, step],
                inner_recv.at[hop, step],
            )

    def arrived(place, recv_sem):
        pltpu.make_async_copy(place, place, recv_sem).wait()

    def group(head, hop):
        return gathered.at[head, pl.ds(pl.multiple_of(origin_outer(hop) * inner, inner), inner)]

    for hop in range(1, outer):
        send(
            own_share, gathered.at[my_head, me], (outer_peer(hop), my_head), outer_send.at[hop], outer_recv.at[hop]
        )
    to_inner(0, own_share)

    for load in loads[:6]:
        load.wait()
    for index in range(2):
        vectors[index] = jnp.zeros((pad, heads * width), F32)
        for h in range(heads):
            vectors[index, h : h + 1, h * width : (h + 1) * width] = score_buf[index, h : h + 1, :]
    source_rows = split_rows(vectors[0])
    target_rows = split_rows(vectors[1])
    mine = jnp.dot(own_buf[...], proj_buf[...], preferred_element_type=F32).astype(BF16)
    own_proj[...] = mine

    def own_terms(rows):
        terms = lax.dot_general(mine, rows, ACROSS, preferred_element_type=F32)
        return terms[:, 0:pad] + terms[:, pad : 2 * pad] + terms[:, 2 * pad : 3 * pad]

    target_terms = own_terms(target_rows)
    self_terms = own_terms(source_rows)

    seen = jnp.int32(0)
    ids = [jnp.int32(0)] * slots
    for j in range(nodes):
        seen = seen + presence_buf[0, j]
        for k in range(slots):
            ids[k] = ids[k] + jnp.minimum(jnp.maximum(k + 1 - seen, 0), 1)

    row = lax.broadcasted_iota(jnp.int32, (tile, tile), 0)
    column = lax.broadcasted_iota(jnp.int32, (tile, tile), 1)
    diagonal = (row == column).astype(jnp.int32)
    for k in range(slots):
        own = 1 - jnp.minimum(jnp.maximum(ids[k] - me, me - ids[k]), 1)
        cut_buf[:, k * tile : (k + 1) * tile] = jnp.where(mask_buf[k] - diagonal * own == 1, 0.0, CUT)

    for hop in range(1, outer):
        place = gathered.at[my_head, origin(hop, 0)]
        arrived(place, outer_recv.at[hop])
        to_inner(hop, place)
    loads[6].wait()

    def group_copy(hop, turn):
        return pltpu.make_async_remote_copy(
            src_ref=group(my_head, hop),
            dst_ref=group(my_head, hop),
            send_sem=group_send.at[hop, turn],
            recv_sem=group_recv.at[hop, turn],
            device_id=(me, head_peer(turn)),
            device_id_type=MESH,
        )

    def project(head, hop):
        first = pl.multiple_of(origin_outer(hop) * inner, inner)
        rows = gathered[head, pl.ds(first, inner)].reshape(inner * share, -1)
        values = jnp.dot(rows, proj_buf[...], preferred_element_type=F32).astype(BF16)
        projected[head, pl.ds(first, inner)] = values.reshape(inner, share, -1)

    def pass_on(hop, carry):
        for step in range(1, inner):
            arrived(gathered.at[my_head, origin(hop, step)], inner_recv.at[hop, step])
        for turn in range(1, heads_dev):
            group_copy(hop, turn).start()
        project(my_head, hop)
        return carry

    lax.fori_loop(0, outer, pass_on, 0)

    def take_in(hop, carry):
        for turn in range(1, heads_dev):
            head = lax.rem(my_head + heads_dev - turn, heads_dev)
            arrived(group(head, hop), group_recv.at[hop, turn])
            project(head, hop)
        return carry

    lax.fori_loop(0, outer, take_in, 0)

    for k in range(slots):
        index = jnp.minimum(ids[k], nodes - 1)
        for head in range(heads_dev):
            first = k * tile + head * share
            source_proj[first : first + share, :] = projected[head, index]
    terms = lax.dot_general(source_rows, source_proj[...], ACROSS, preferred_element_type=F32)
    source_terms = terms[0:pad] + terms[pad : 2 * pad] + terms[2 * pad : 3 * pad]

    heads_out = []
    for h in range(heads):
        lanes = slice(h * width, (h + 1) * width)
        target = jnp.broadcast_to(target_terms[:, h : h + 1], (tile, tile))
        itself = jnp.broadcast_to(self_terms[:, h : h + 1], (tile, tile))
        reach = [
            source_terms[h : h + 1, k * tile : (k + 1) * tile] + cut_buf[:, k * tile : (k + 1) * tile]
            for k in range(slots)
        ]
        best = jnp.max(functools.reduce(jnp.maximum, reach, itself), axis=1, keepdims=True)
        peak = leaky_relu(target + best)
        weights = [jnp.exp(leaky_relu(target + values) - peak) for values in reach]
        self_weight = jnp.exp(leaky_relu(target + itself) - peak)
        denominator = jnp.sum(functools.reduce(jnp.add, weights), axis=1, keepdims=True) + self_weight[:, :1]
        self_weight = self_weight[:, :1]
        rounded = jnp.concatenate([values.astype(BF16) for values in weights], axis=1)
        total = jnp.dot(rounded, source_proj[:, lanes], preferred_element_type=F32)
        total = total + self_weight.astype(BF16).astype(F32) * own_proj[:, lanes].astype(F32)
        heads_out.append(elu(total * (1.0 / denominator)).astype(BF16))
    loads[7].wait()
    joined = jnp.concatenate(heads_out, axis=1)
    partials[my_head] = jnp.dot(joined, out_buf[...], preferred_element_type=F32).astype(BF16)

    for turn in range(1, heads_dev):
        send(
            partials.at[my_head], partials.at[my_head], (me, head_peer(turn)), part_send.at[turn], part_recv.at[turn]
        )
    for turn in range(1, heads_dev):
        source = lax.rem(my_head + heads_dev - turn, heads_dev)
        arrived(partials.at[source], part_recv.at[turn])
    total = partials[0].astype(F32)
    for index in range(1, heads_dev):
        total = total + partials[index].astype(F32)
    result[...] = total.astype(BF16)
    for copy in started:
        copy.wait_send()
    for hop in range(outer):
        for turn in range(1, heads_dev):
            group_copy(hop, turn).wait_send()


def per_device(nodes, heads_dev, features, proj_weight, score_source, score_target, out_weight, presence, tile_masks):
    tile = features.shape[0]
    heads, width = score_source.shape
    slots = tile_masks.shape[1]
    outputs = out_weight.shape[1]
    inner = 1
    while inner * inner * 4 <= nodes:
        inner *= 2
    outer = nodes // inner
    pad = -(-heads // 8) * 8
    sizes = (outer, inner, heads_dev, heads, width, tile, slots)
    dma = pltpu.SemaphoreType.DMA
    return pl.pallas_call(
        functools.partial(kernel, sizes),
        out_shape=jax.ShapeDtypeStruct((tile, outputs), BF16),
        in_specs=[pl.BlockSpec(memory_space=pltpu.HBM)] * 7,
        out_specs=pl.BlockSpec(memory_space=pltpu.VMEM),
        scratch_shapes=[
            pltpu.VMEM((heads_dev, nodes, tile // heads_dev, features.shape[1]), BF16),
            pltpu.VMEM(features.shape, BF16),
            pltpu.VMEM(proj_weight.shape, BF16),
            pltpu.VMEM((2, heads, width), F32),
            pltpu.VMEM(out_weight.shape, BF16),
            pltpu.SMEM(presence.shape, jnp.int32),
            pltpu.VMEM(tile_masks.shape[1:], jnp.int32),
            pltpu.VMEM((tile, slots * tile), F32),
            pltpu.VMEM((2, pad, heads * width), F32),
            pltpu.VMEM((tile, heads * width), BF16),
            pltpu.VMEM((heads_dev, nodes, tile // heads_dev, heads * width), BF16),
            pltpu.VMEM((slots * tile, heads * width), BF16),
            pltpu.VMEM((heads_dev, tile, outputs), BF16),
            dma((8,)),
            dma((outer,)),
            dma((outer,)),
            dma((outer, inner)),
            dma((outer, inner)),
            dma((outer, heads_dev)),
            dma((outer, heads_dev)),
            dma((heads_dev,)),
            dma((heads_dev,)),
        ],
        compiler_params=pltpu.CompilerParams(
            collective_id=0, has_side_effects=True, vmem_limit_bytes=48 * 1024 * 1024
        ),
        cost_estimate=pl.CostEstimate(
            flops=2 * tile * heads * width * (features.shape[1] + outputs)
            + 2 * slots * tile * heads * width * (features.shape[1] + tile),
            bytes_accessed=4 * slots * tile * tile + 2 * nodes * tile * features.shape[1],
            transcendentals=slots * tile * tile * heads,
        ),
    )(
        *(
            pltpu.with_memory_space_constraint(operand, pltpu.HBM)
            for operand in (features, proj_weight, score_source, score_target, out_weight, presence, tile_masks)
        )
    )


def solution(mesh):
    return jax.shard_map(
        functools.partial(per_device, mesh.shape["node"], mesh.shape["head"]),
        mesh=mesh,
        in_specs=(
            P("node", None),
            P(None, "head"),
            P("head", None),
            P("head", None),
            P("head", None),
            P("node", None),
            P("node", None, None, None),
        ),
        out_specs=P("node", None),
        check_vma=False,
    )
```

profile of v0, /device:TPU:0, one launch (start us, length us, event | category | flops | bytes accessed | tf_op | source)
XLA Modules:
  0.0 17.3 jit_solution(6764235027976914125)
XLA Ops:
  0.0 16.7 %shard_map.73 = bf16[128,256]{1,0:T(8,128)(2,1)S(1)} custom-call(bf16[128,128]{1,0:T(8,128)(2,1)} %features.1, bf16[128,512]{1,0:T(8,128)(2,1)} %proj_weight.1, f32[4,128]{1,0:T(4,128)} %score_source.1, f32[4,128]{1,0:T(4,128)} %score_target.1, bf16[512,256]{1,0:T(8,128)(2,1)} %out_weight.1, s32[1,16]{1,0:T(1,128)} %presence.1, s32[1,4,128,128]{3,2,1,0:T(8,128)} %tile_masks.1), custom_call_target="tpu_custom_call" | custom-call | flops 184549376 | bytes 786432 | tf_op jit(solution)/shard_map/pallas_call | solution.py:288
  16.7 0.6 %copy.9 = bf16[128,256]{1,0:T(8,128)(2,1)} copy(bf16[128,256]{1,0:T(8,128)(2,1)S(1)} %shard_map.73) | data formatting | bytes 131072
where the time goes:
time: 17.4 us; the launch traced here: 17.3 us
  Pallas kernels  16.7 us (96%)
  local copies, waits for them, and re-layouts  0.63 us (4%)
    pallas_call x1, Pallas kernels, per_device(): pl.pallas_call(functools.partial(kernel, sizes), out_shape=jax.ShapeDtype...  16.7 us
    unnamed x1, local copies, waits for them, and re-layouts  0.63 us

commit v1 on v0

--- a/solution.py
+++ b/solution.py
@@ -75,11 +75,19 @@
     my_inner = me % inner
     share = tile // heads_dev
 
+    def paired(position, step, size):
+        other = 0
+        bit = 1
+        while bit < size:
+            other = other + bit * ((position // bit + step // bit) % 2)
+            bit *= 2
+        return other
+
     def outer_peer(step):
-        return lax.rem(my_outer + step, outer) * inner + my_inner
+        return paired(my_outer, step, outer) * inner + my_inner
 
     def inner_peer(step):
-        return my_outer * inner + lax.rem(my_inner + step, inner)
+        return my_outer * inner + paired(my_inner, step, inner)
 
     def head_peer(step):
         return lax.rem(my_head + step, heads_dev)
@@ -93,6 +101,50 @@
         pl.semaphore_signal(barrier, inc=1, device_id=(me, head_peer(step)), device_id_type=MESH)
 
     own_share = features.at[pl.ds(pl.multiple_of(my_head * share, share), share), :]
+    pl.semaphore_wait(barrier, outer + inner + heads_dev - 3)
+
+    started = []
+
+    def send(source, target, to, send_sem, recv_sem):
+        copy = pltpu.make_async_remote_copy(
+            src_ref=source,
+            dst_ref=target,
+            send_sem=send_sem,
+            recv_sem=recv_sem,
+            device_id=to,
+            device_id_type=MESH,
+        )
+        copy.start()
+        started.append(copy)
+
+    def origin_outer(hop):
+        return paired(my_outer, hop, outer)
+
+    def origin(hop, step):
+        return origin_outer(hop) * inner + paired(my_inner, step, inner)
+
+    def to_inner(hop, source):
+        for step in reversed(range(1, inner)):
+            send(
+                source,
+                gathered.at[my_head, origin(hop, 0)],
+                (inner_peer(step), my_head),
+                inner_send.at[hop, step],
+                inner_recv.at[hop, step],
+            )
+
+    def arrived(place, recv_sem):
+        pltpu.make_async_copy(place, place, recv_sem).wait()
+
+    def group(head, hop):
+        return gathered.at[head, pl.ds(pl.multiple_of(origin_outer(hop) * inner, inner), inner)]
+
+    for hop in range(1, outer):
+        send(
+            own_share, gathered.at[my_head, me], (outer_peer(hop), my_head), outer_send.at[hop], outer_recv.at[hop]
+        )
+    to_inner(0, own_share)
+
     loads = []
     for source, target in (
         (features, own_buf),
@@ -107,49 +159,11 @@
         load = pltpu.make_async_copy(source, target, local_sem.at[len(loads)])
         load.start()
         loads.append(load)
-    pl.semaphore_wait(barrier, outer + inner + heads_dev - 3)
-
-    started = []
-
-    def send(source, target, to, send_sem, recv_sem):
-        copy = pltpu.make_async_remote_copy(
-            src_ref=source,
-            dst_ref=target,
-            send_sem=send_sem,
-            recv_sem=recv_sem,
-            device_id=to,
-            device_id_type=MESH,
-        )
-        copy.start()
-        started.append(copy)
-
-    def origin_outer(hop):
-        return lax.rem(my_outer + outer - hop, outer)
-
-    def origin(hop, step):
-        return origin_outer(hop) * inner + lax.rem(my_inner + inner - step, inner)
-
-    def to_inner(hop, source):
-        for step in range(1, inner):
-            send(
-                source,
-                gathered.at[my_head, origin(hop, 0)],
-                (inner_peer(step), my_head),
-                inner_send.at[hop, step],
-                inner_recv.at[hop, step],
-            )
-
-    def arrived(place, recv_sem):
-        pltpu.make_async_copy(place, place, recv_sem).wait()
-
-    def group(head, hop):
-        return gathered.at[head, pl.ds(pl.multiple_of(origin_outer(hop) * inner, inner), inner)]
 
     for hop in range(1, outer):
-        send(
-            own_share, gathered.at[my_head, me], (outer_peer(hop), my_head), outer_send.at[hop], outer_recv.at[hop]
-        )
-    to_inner(0, own_share)
+        place = gathered.at[my_head, origin(hop, 0)]
+        arrived(place, outer_recv.at[hop])
+        to_inner(hop, place)
 
     for load in loads[:6]:
         load.wait()
@@ -183,10 +197,6 @@
         own = 1 - jnp.minimum(jnp.maximum(ids[k] - me, me - ids[k]), 1)
         cut_buf[:, k * tile : (k + 1) * tile] = jnp.where(mask_buf[k] - diagonal * own == 1, 0.0, CUT)
 
-    for hop in range(1, outer):
-        place = gathered.at[my_head, origin(hop, 0)]
-        arrived(place, outer_recv.at[hop])
-        to_inner(hop, place)
     loads[6].wait()
 
     def group_copy(hop, turn):
@@ -282,6 +292,7 @@
     while inner * inner * 4 <= nodes:
         inner *= 2
     outer = nodes // inner
+    assert outer & (outer - 1) == 0
     pad = -(-heads // 8) * 8
     sizes = (outer, inner, heads_dev, heads, width, tile, slots)
     dma = pltpu.SemaphoreType.DMA

time: 17.4 us -> 17.4 us (level)
  no operation moved by 1% of the time
where the time goes in v1:
time: 17.4 us; the launch traced here: 17.3 us
  Pallas kernels  16.7 us (96%)
  local copies, waits for them, and re-layouts  0.63 us (4%)
    pallas_call x1, Pallas kernels, per_device(): pl.pallas_call(functools.partial(kernel, sizes), out_shape=jax.ShapeDtype...  16.7 us
    unnamed x1, local copies, waits for them, and re-layouts  0.63 us

profile of v1, /device:TPU:0, one launch (start us, length us, event | category | flops | bytes accessed | tf_op | source)
XLA Modules:
  0.0 17.3 jit_solution(7434642189458353513)
XLA Ops:
  0.0 16.7 %shard_map.73 = bf16[128,256]{1,0:T(8,128)(2,1)S(1)} custom-call(bf16[128,128]{1,0:T(8,128)(2,1)} %features.1, bf16[128,512]{1,0:T(8,128)(2,1)} %proj_weight.1, f32[4,128]{1,0:T(4,128)} %score_source.1, f32[4,128]{1,0:T(4,128)} %score_target.1, bf16[512,256]{1,0:T(8,128)(2,1)} %out_weight.1, s32[1,16]{1,0:T(1,128)} %presence.1, s32[1,4,128,128]{3,2,1,0:T(8,128)} %tile_masks.1), custom_call_target="tpu_custom_call" | custom-call | flops 184549376 | bytes 786432 | tf_op jit(solution)/shard_map/pallas_call | solution.py:299
  16.7 0.6 %copy.9 = bf16[128,256]{1,0:T(8,128)(2,1)} copy(bf16[128,256]{1,0:T(8,128)(2,1)S(1)} %shard_map.73) | data formatting | bytes 131072

commit v2 on v1

--- a/solution.py
+++ b/solution.py
@@ -55,6 +55,10 @@
     own_proj,
     projected,
     source_proj,
+    spread,
+    source_terms,
+    rounded,
+    scales,
     partials,
     local_sem,
     outer_send,
@@ -74,6 +78,7 @@
     my_outer = me // inner
     my_inner = me % inner
     share = tile // heads_dev
+    chunk = min(tile, 32)
 
     def paired(position, step, size):
         other = 0
@@ -180,8 +185,10 @@
         terms = lax.dot_general(mine, rows, ACROSS, preferred_element_type=F32)
         return terms[:, 0:pad] + terms[:, pad : 2 * pad] + terms[:, 2 * pad : 3 * pad]
 
-    target_terms = own_terms(target_rows)
-    self_terms = own_terms(source_rows)
+    for index, rows in enumerate((target_rows, source_rows)):
+        terms = own_terms(rows)
+        for h in range(heads):
+            spread[index, h] = jnp.broadcast_to(terms[:, h : h + 1], (tile, tile))
 
     seen = jnp.int32(0)
     ids = [jnp.int32(0)] * slots
@@ -240,27 +247,37 @@
             first = k * tile + head * share
             source_proj[first : first + share, :] = projected[head, index]
     terms = lax.dot_general(source_rows, source_proj[...], ACROSS, preferred_element_type=F32)
-    source_terms = terms[0:pad] + terms[pad : 2 * pad] + terms[2 * pad : 3 * pad]
+    source_terms[...] = terms[0:pad] + terms[pad : 2 * pad] + terms[2 * pad : 3 * pad]
+
+    def weigh(index, carry):
+        lines = pl.ds(pl.multiple_of(index * chunk, chunk), chunk)
+        for h in range(heads):
+            target = spread[0, h, lines, :]
+            itself = spread[1, h, lines, :]
+            reach = [
+                source_terms[h : h + 1, k * tile : (k + 1) * tile] + cut_buf[lines, k * tile : (k + 1) * tile]
+                for k in range(slots)
+            ]
+            best = jnp.max(functools.reduce(jnp.maximum, reach, itself), axis=1, keepdims=True)
+            peak = leaky_relu(target + best)
+            weights = [jnp.exp(leaky_relu(target + values) - peak) for values in reach]
+            self_weight = jnp.exp(leaky_relu(target + itself) - peak)
+            denominator = jnp.sum(functools.reduce(jnp.add, weights), axis=1, keepdims=True) + self_weight
+            for k in range(slots):
+                rounded[h, lines, k * tile : (k + 1) * tile] = weights[k].astype(BF16)
+            scales[0, h, lines, :] = 1.0 / denominator
+            scales[1, h, lines, :] = self_weight
+        return carry
+
+    lax.fori_loop(0, tile // chunk, weigh, 0)
 
     heads_out = []
     for h in range(heads):
         lanes = slice(h * width, (h + 1) * width)
-        target = jnp.broadcast_to(target_terms[:, h : h + 1], (tile, tile))
-        itself = jnp.broadcast_to(self_terms[:, h : h + 1], (tile, tile))
-        reach = [
-            source_terms[h : h + 1, k * tile : (k + 1) * tile] + cut_buf[:, k * tile : (k + 1) * tile]
-            for k in range(slots)
-        ]
-        best = jnp.max(functools.reduce(jnp.maximum, reach, itself), axis=1, keepdims=True)
-        peak = leaky_relu(target + best)
-        weights = [jnp.exp(leaky_relu(target + values) - peak) for values in reach]
-        self_weight = jnp.exp(leaky_relu(target + itself) - peak)
-        denominator = jnp.sum(functools.reduce(jnp.add, weights), axis=1, keepdims=True) + self_weight[:, :1]
-        self_weight = self_weight[:, :1]
-        rounded = jnp.concatenate([values.astype(BF16) for values in weights], axis=1)
-        total = jnp.dot(rounded, source_proj[:, lanes], preferred_element_type=F32)
-        total = total + self_weight.astype(BF16).astype(F32) * own_proj[:, lanes].astype(F32)
-        heads_out.append(elu(total * (1.0 / denominator)).astype(BF16))
+        total = jnp.dot(rounded[h], source_proj[:, lanes], preferred_element_type=F32)
+        self_weight = scales[1, h][:, :width].astype(BF16).astype(F32)
+        total = total + self_weight * own_proj[:, lanes].astype(F32)
+        heads_out.append(elu(total * scales[0, h][:, :width]).astype(BF16))
     loads[7].wait()
     joined = jnp.concatenate(heads_out, axis=1)
     partials[my_head] = jnp.dot(joined, out_buf[...], preferred_element_type=F32).astype(BF16)
@@ -292,6 +309,7 @@
     while inner * inner * 4 <= nodes:
         inner *= 2
     outer = nodes // inner
+    assert width <= tile
     assert outer & (outer - 1) == 0
     pad = -(-heads // 8) * 8
     sizes = (outer, inner, heads_dev, heads, width, tile, slots)
@@ -314,6 +332,10 @@
             pltpu.VMEM((tile, heads * width), BF16),
             pltpu.VMEM((heads_dev, nodes, tile // heads_dev, heads * width), BF16),
             pltpu.VMEM((slots * tile, heads * width), BF16),
+            pltpu.VMEM((2, heads, tile, tile), F32),
+            pltpu.VMEM((pad, slots * tile), F32),
+            pltpu.VMEM((heads, tile, slots * tile), BF16),
+            pltpu.VMEM((2, heads, tile, tile), F32),
             pltpu.VMEM((heads_dev, tile, outputs), BF16),
             dma((8,)),
             dma((outer,)),

time: 17.4 us -> 18 us (1.034)
  Pallas kernels: 16.7 us -> 17.2 us
    pallas_call x1, Pallas kernels: 16.7 us -> 17.2 us  [per_device(): pl.pallas_call(functools.partial(kernel, sizes), out_shape=jax.ShapeDtype...]
where the time goes in v2:
time: 18 us; the launch traced here: 17.8 us
  Pallas kernels  17.2 us (96%)
  local copies, waits for them, and re-layouts  0.63 us (4%)
    pallas_call x1, Pallas kernels, per_device(): pl.pallas_call(functools.partial(kernel, sizes), out_shape=jax.ShapeDtype...  17.2 us
    unnamed x1, local copies, waits for them, and re-layouts  0.63 us

profile of v2, /device:TPU:0, one launch (start us, length us, event | category | flops | bytes accessed | tf_op | source)
XLA Modules:
  0.0 17.8 jit_solution(3004017802997871797)
XLA Ops:
  0.0 17.2 %shard_map.73 = bf16[128,256]{1,0:T(8,128)(2,1)S(1)} custom-call(bf16[128,128]{1,0:T(8,128)(2,1)} %features.1, bf16[128,512]{1,0:T(8,128)(2,1)} %proj_weight.1, f32[4,128]{1,0:T(4,128)} %score_source.1, f32[4,128]{1,0:T(4,128)} %score_target.1, bf16[512,256]{1,0:T(8,128)(2,1)} %out_weight.1, s32[1,16]{1,0:T(1,128)} %presence.1, s32[1,4,128,128]{3,2,1,0:T(8,128)} %tile_masks.1), custom_call_target="tpu_custom_call" | custom-call | flops 184549376 | bytes 786432 | tf_op jit(solution)/shard_map/pallas_call | solution.py:317
  17.2 0.6 %copy.9 = bf16[128,256]{1,0:T(8,128)(2,1)} copy(bf16[128,256]{1,0:T(8,128)(2,1)S(1)} %shard_map.73) | data formatting | bytes 131072

commit v3 on v1

--- a/solution.py
+++ b/solution.py
@@ -44,6 +44,7 @@
     tile_masks,
     result,
     gathered,
+    others,
     own_buf,
     proj_buf,
     score_buf,
@@ -53,7 +54,6 @@
     cut_buf,
     vectors,
     own_proj,
-    projected,
     source_proj,
     partials,
     local_sem,
@@ -127,7 +127,7 @@
         for step in reversed(range(1, inner)):
             send(
                 source,
-                gathered.at[my_head, origin(hop, 0)],
+                gathered.at[origin(hop, 0)],
                 (inner_peer(step), my_head),
                 inner_send.at[hop, step],
                 inner_recv.at[hop, step],
@@ -136,12 +136,12 @@
     def arrived(place, recv_sem):
         pltpu.make_async_copy(place, place, recv_sem).wait()
 
-    def group(head, hop):
-        return gathered.at[head, pl.ds(pl.multiple_of(origin_outer(hop) * inner, inner), inner)]
+    def group(place, hop):
+        return place.at[pl.ds(pl.multiple_of(origin_outer(hop) * inner, inner), inner)]
 
     for hop in range(1, outer):
         send(
-            own_share, gathered.at[my_head, me], (outer_peer(hop), my_head), outer_send.at[hop], outer_recv.at[hop]
+            own_share, gathered.at[me], (outer_peer(hop), my_head), outer_send.at[hop], outer_recv.at[hop]
         )
     to_inner(0, own_share)
 
@@ -153,7 +153,7 @@
         (score_target, score_buf.at[1]),
         (presence, presence_buf),
         (tile_masks.at[0], mask_buf),
-        (own_share, gathered.at[my_head, me]),
+        (own_share, gathered.at[me]),
         (out_weight, out_buf),
     ):
         load = pltpu.make_async_copy(source, target, local_sem.at[len(loads)])
@@ -161,7 +161,7 @@
         loads.append(load)
 
     for hop in range(1, outer):
-        place = gathered.at[my_head, origin(hop, 0)]
+        place = gathered.at[origin(hop, 0)]
         arrived(place, outer_recv.at[hop])
         to_inner(hop, place)
 
@@ -201,44 +201,34 @@
 
     def group_copy(hop, turn):
         return pltpu.make_async_remote_copy(
-            src_ref=group(my_head, hop),
-            dst_ref=group(my_head, hop),
+            src_ref=group(gathered, hop),
+            dst_ref=group(others.at[turn - 1], hop),
             send_sem=group_send.at[hop, turn],
             recv_sem=group_recv.at[hop, turn],
             device_id=(me, head_peer(turn)),
             device_id_type=MESH,
         )
 
-    def project(head, hop):
-        first = pl.multiple_of(origin_outer(hop) * inner, inner)
-        rows = gathered[head, pl.ds(first, inner)].reshape(inner * share, -1)
-        values = jnp.dot(rows, proj_buf[...], preferred_element_type=F32).astype(BF16)
-        projected[head, pl.ds(first, inner)] = values.reshape(inner, share, -1)
-
-    def pass_on(hop, carry):
+    def project(place, head):
+        rows = [place[jnp.minimum(ids[k], nodes - 1)] for k in range(slots)]
+        values = jnp.dot(
+            jnp.concatenate(rows, axis=0), proj_buf[...], preferred_element_type=F32
+        ).astype(BF16)
+        for k in range(slots):
+            first = pl.multiple_of(k * tile + head * share, share)
+            source_proj[pl.ds(first, share), :] = values[k * share : (k + 1) * share]
+
+    for hop in range(outer):
         for step in range(1, inner):
-            arrived(gathered.at[my_head, origin(hop, step)], inner_recv.at[hop, step])
+            arrived(gathered.at[origin(hop, step)], inner_recv.at[hop, step])
         for turn in range(1, heads_dev):
             group_copy(hop, turn).start()
-        project(my_head, hop)
-        return carry
-
-    lax.fori_loop(0, outer, pass_on, 0)
-
-    def take_in(hop, carry):
+    project(gathered, my_head)
+    for hop in range(outer):
         for turn in range(1, heads_dev):
-            head = lax.rem(my_head + heads_dev - turn, heads_dev)
-            arrived(group(head, hop), group_recv.at[hop, turn])
-            project(head, hop)
-        return carry
-
-    lax.fori_loop(0, outer, take_in, 0)
-
-    for k in range(slots):
-        index = jnp.minimum(ids[k], nodes - 1)
-        for head in range(heads_dev):
-            first = k * tile + head * share
-            source_proj[first : first + share, :] = projected[head, index]
+            arrived(group(others.at[turn - 1], hop), group_recv.at[hop, turn])
+    for turn in range(1, heads_dev):
+        project(others.at[turn - 1], lax.rem(my_head + heads_dev - turn, heads_dev))
     terms = lax.dot_general(source_rows, source_proj[...], ACROSS, preferred_element_type=F32)
     source_terms = terms[0:pad] + terms[pad : 2 * pad] + terms[2 * pad : 3 * pad]
 
@@ -265,10 +255,16 @@
     joined = jnp.concatenate(heads_out, axis=1)
     partials[my_head] = jnp.dot(joined, out_buf[...], preferred_element_type=F32).astype(BF16)
 
+    gathers = len(started)
     for turn in range(1, heads_dev):
         send(
             partials.at[my_head], partials.at[my_head], (me, head_peer(turn)), part_send.at[turn], part_recv.at[turn]
         )
+    for copy in started[:gathers]:
+        copy.wait_send()
+    for hop in range(outer):
+        for turn in range(1, heads_dev):
+            group_copy(hop, turn).wait_send()
     for turn in range(1, heads_dev):
         source = lax.rem(my_head + heads_dev - turn, heads_dev)
         arrived(partials.at[source], part_recv.at[turn])
@@ -276,11 +272,8 @@
     for index in range(1, heads_dev):
         total = total + partials[index].astype(F32)
     result[...] = total.astype(BF16)
-    for copy in started:
+    for copy in started[gathers:]:
         copy.wait_send()
-    for hop in range(outer):
-        for turn in range(1, heads_dev):
-            group_copy(hop, turn).wait_send()
 
 
 def per_device(nodes, heads_dev, features, proj_weight, score_source, score_target, out_weight, presence, tile_masks):
@@ -302,7 +295,8 @@
         in_specs=[pl.BlockSpec(memory_space=pltpu.HBM)] * 7,
         out_specs=pl.BlockSpec(memory_space=pltpu.VMEM),
         scratch_shapes=[
-            pltpu.VMEM((heads_dev, nodes, tile // heads_dev, features.shape[1]), BF16),
+            pltpu.VMEM((nodes, tile // heads_dev, features.shape[1]), BF16),
+            pltpu.VMEM((heads_dev - 1, nodes, tile // heads_dev, features.shape[1]), BF16),
             pltpu.VMEM(features.shape, BF16),
             pltpu.VMEM(proj_weight.shape, BF16),
             pltpu.VMEM((2, heads, width), F32),
@@ -312,7 +306,6 @@
             pltpu.VMEM((tile, slots * tile), F32),
             pltpu.VMEM((2, pad, heads * width), F32),
             pltpu.VMEM((tile, heads * width), BF16),
-            pltpu.VMEM((heads_dev, nodes, tile // heads_dev, heads * width), BF16),
             pltpu.VMEM((slots * tile, heads * width), BF16),
             pltpu.VMEM((heads_dev, tile, outputs), BF16),
             dma((8,)),

time: 17.4 us -> 17.4 us (level)
  no operation moved by 1% of the time
where the time goes in v3:
time: 17.4 us; the launch traced here: 17.3 us
  Pallas kernels  16.6 us (95%)
  local copies, waits for them, and re-layouts  0.63 us (4%)
    pallas_call x1, Pallas kernels, per_device(): pl.pallas_call(functools.partial(kernel, sizes), out_shape=jax.ShapeDtype...  16.6 us
    unnamed x1, local copies, waits for them, and re-layouts  0.63 us

profile of v3, /device:TPU:0, one launch (start us, length us, event | category | flops | bytes accessed | tf_op | source)
XLA Modules:
  0.0 17.3 jit_solution(7843401911348370507)
XLA Ops:
  0.0 16.6 %shard_map.73 = bf16[128,256]{1,0:T(8,128)(2,1)S(1)} custom-call(bf16[128,128]{1,0:T(8,128)(2,1)} %features.1, bf16[128,512]{1,0:T(8,128)(2,1)} %proj_weight.1, f32[4,128]{1,0:T(4,128)} %score_source.1, f32[4,128]{1,0:T(4,128)} %score_target.1, bf16[512,256]{1,0:T(8,128)(2,1)} %out_weight.1, s32[1,16]{1,0:T(1,128)} %presence.1, s32[1,4,128,128]{3,2,1,0:T(8,128)} %tile_masks.1), custom_call_target="tpu_custom_call" | custom-call | flops 184549376 | bytes 786432 | tf_op jit(solution)/shard_map/pallas_call | solution.py:292
  16.6 0.6 %copy.9 = bf16[128,256]{1,0:T(8,128)(2,1)} copy(bf16[128,256]{1,0:T(8,128)(2,1)S(1)} %shard_map.73) | data formatting | bytes 131072
